TPU v7x, 512 devices: a whole 4x8x8 slice. The times are simulated.
512 devices in a mesh: ctx: 64 (over y, x, core), tp: 8 (over z).
Axes of the slice: x: 4, y: 8, z: 8, core: 2. Of those that a mesh axis runs over, the one named last changes fastest.
Arguments:
- queries: bfloat16 [32768, 4096], P('ctx', 'tp'), may hold values from -8 to 8
- keys: bfloat16 [32768, 4096], P('ctx', 'tp'), may hold values from -6 to 6
- values: bfloat16 [32768, 4096], P('ctx', 'tp'), may hold values from -6 to 6
- log_decay: float32 [32768, 32], P('ctx', 'tp'), may hold values from -4 to 0
- gain: float32 [4096], P('tp'), may hold values from 0.1 to 1.9
- upstream: bfloat16 [32768, 4096], P('ctx', 'tp'), may hold values from -40 to 40
Outputs:
- attn_out: bfloat16 [32768, 4096], P('ctx', 'tp')
- grad_queries: bfloat16 [32768, 4096], P('ctx', 'tp')
- grad_keys: bfloat16 [32768, 4096], P('ctx', 'tp')
- grad_values: bfloat16 [32768, 4096], P('ctx', 'tp')
- grad_gain: float32 [4096], P('tp')
All inputs are finite; a program needn't handle non-finite values.
Results may differ from a plain program's by a relative error of at most 0.0051.
Values sent between devices are 32-bit elements; how exact they have to be, the bound alone decides.
A program may use at most 128 MiB of HBM per device.

v0:
```python
import jax
import jax.numpy as jnp
from jax import lax
from jax.sharding import PartitionSpec as P

BLK = 512
FEAT = 4096


def entering_2(part, axis, combine, identity):
    count = lax.axis_size(axis)
    place = lax.axis_index(axis)
    ahead = count - 1 - place
    gathered = jax.tree.map(lambda a: lax.all_gather(a, axis), part)
    state = jax.tree.map(lambda a, e: jnp.zeros_like(a) + jnp.asarray(e, a.dtype), part, identity)

    def one(hop, state):
        source = count - 1 - hop
        return combine(
            state, jax.tree.map(lambda a: lax.dynamic_index_in_dim(a, source, 0, False), gathered)
        )

    return lax.fori_loop(0, ahead, one, state)


def block_weights(lam_block, lower_mask):
    cum_log = jnp.cumsum(lam_block, axis=0)
    trans = cum_log.T
    diff = trans[:, :, None] - trans[:, None, :]
    return (cum_log, jnp.exp(jnp.where(lower_mask[None], diff, -jnp.inf)))


def chain_link(earlier, later):
    return (earlier[0] * later[0], later[0][:, None, None] * earlier[1] + later[1])


def body(queries, keys, values, log_decay, gain, upstream):
    highest = lax.Precision.HIGHEST
    f32 = jnp.float32
    tok_dev = queries.shape[0]
    head_dev = log_decay.shape[1]
    head_width = queries.shape[1] // head_dev
    count = tok_dev // BLK
    query_heads = queries.reshape(tok_dev, head_dev, head_width)
    key_heads = keys.reshape(tok_dev, head_dev, head_width)
    value_heads = values.reshape(tok_dev, head_dev, head_width)
    offsets = jnp.arange(BLK)
    lower_mask = offsets[:, None] >= offsets[None, :]
    cums, weights, score_list, inside_list, local_list, decay_list = ([], [], [], [], [], [])
    kk = key_heads
    vv = value_heads
    cum_log, weight_mat = block_weights(log_decay, lower_mask)
    last = cum_log[-1]
    raw_scores = jnp.einsum("ihd,jhd->hij", query_heads, kk, preferred_element_type=f32)
    scores = (raw_scores * weight_mat).astype(jnp.bfloat16)
    inside = jnp.einsum("hij,jhd->ihd", scores, vv, preferred_element_type=f32)
    keyed_rows = kk.astype(f32) * jnp.exp(last[None, :] - cum_log)[:, :, None]
    local_state = jnp.einsum("jhd,jhe->hde", keyed_rows, vv.astype(f32), precision=highest)
    cums.append(cum_log)
    weights.append(weight_mat)
    score_list.append(scores)
    inside_list.append(inside)
    local_list.append(local_state)
    decay_list.append(jnp.exp(last))
    total_decay = jnp.ones((head_dev,), f32)
    total_state = jnp.zeros((head_dev, head_width, head_width), f32)
    b = 0
    total_state = decay_list[b][:, None, None] * total_state + local_list[b]
    total_decay = total_decay * decay_list[b]
    log_total = cums[b][-1]
    identity = (jnp.ones((head_dev,), f32), jnp.zeros((head_dev, head_width, head_width), f32))
    all_logs = lax.all_gather(log_total[None, :], "ctx", axis=0, tiled=True)
    inclusive = jnp.cumsum(all_logs, axis=0)
    mine = lax.axis_index("ctx")
    before = lax.dynamic_index_in_dim(
        inclusive, mine, 0, keepdims=False
    ) - lax.dynamic_index_in_dim(all_logs, mine, 0, keepdims=False)
    piece = lax.all_gather(total_state[None], "ctx", axis=0, tiled=True)
    rows_here = piece.shape[0]
    index_rows = jnp.arange(rows_here)
    gap = before[None, :] - inclusive
    factor = jnp.exp(jnp.where((index_rows < mine)[:, None], gap, -jnp.inf))
    incoming = jnp.einsum("nh,nhde->hde", factor, piece, precision=highest)
    acts, entering = ([], [])
    b = 0
    entering.append(incoming)
    outer = jnp.exp(cums[b])[:, :, None] * jnp.einsum(
        "ihd,hde->ihe", query_heads.astype(f32), incoming, precision=highest
    )
    acts.append(inside_list[b] + outer)
    attended = acts[0].reshape(tok_dev, head_dev * head_width)
    gain_row = gain[None, :]
    up_grad = upstream.astype(f32)
    scaled = gain_row * up_grad
    square_sum, cross_sum = lax.psum(
        (jnp.sum(attended * attended, axis=1), jnp.sum(attended * scaled, axis=1)), "tp"
    )
    inv_rms = lax.rsqrt(square_sum / FEAT + 1e-06)[:, None]
    normed = attended * inv_rms
    attn_out = (normed * gain_row).astype(jnp.bfloat16)
    grad_gain = lax.psum(jnp.sum(normed * up_grad, axis=0), "ctx")
    cross_mean = (cross_sum / FEAT)[:, None]
    grad_attn = (inv_rms * scaled - attended * (inv_rms * inv_rms * inv_rms) * cross_mean).astype(
        jnp.bfloat16
    )
    grad_heads = grad_attn.reshape(tok_dev, head_dev, head_width)
    prefix = jnp.ones((head_dev,), f32)
    device_moment = identity[1]
    b = 0
    dd = grad_heads
    moment = jnp.einsum(
        "ihd,ihe->hde",
        query_heads.astype(f32) * jnp.exp(cums[b])[:, :, None],
        dd.astype(f32),
        precision=highest,
    )
    moments = [moment]
    device_moment = prefix[:, None, None] * moment
    b = 0
    kk = key_heads
    vv = value_heads
    dd = grad_heads
    raw_grad = jnp.einsum("ihe,jhe->hij", dd, vv, preferred_element_type=f32)
    grad_mat = (raw_grad * weights[b]).astype(jnp.bfloat16)
    grad_q = jnp.einsum("hij,jhd->ihd", grad_mat, kk, preferred_element_type=f32)
    grad_k = jnp.einsum("hij,ihd->jhd", grad_mat, query_heads, preferred_element_type=f32)
    grad_v = jnp.einsum("hij,ihe->jhe", score_list[b], dd, preferred_element_type=f32)
    inner_parts = [(grad_q, grad_k, grad_v)]
    back_state = entering_2((total_decay, device_moment), "ctx", chain_link, identity)[1]
    grad_end = back_state
    q_parts, k_parts, v_parts = ([None] * count, [None] * count, [None] * count)
    for b in reversed(range(count)):
        kk = key_heads
        vv = value_heads
        dd = grad_heads
        cum_log = cums[b]
        rise = jnp.exp(cum_log)[:, :, None]
        fall = jnp.exp(cum_log[-1][None, :] - cum_log)[:, :, None]
        grad_q, grad_k, grad_v = inner_parts[b]
        q_parts[b] = grad_q + rise * jnp.einsum(
            "ihe,hde->ihd", dd.astype(f32), entering[b], precision=highest
        )
        k_parts[b] = grad_k + fall * jnp.einsum(
            "jhe,hde->jhd", vv.astype(f32), grad_end, precision=highest
        )
        v_parts[b] = grad_v + fall * jnp.einsum(
            "jhd,hde->jhe", kk.astype(f32), grad_end, precision=highest
        )
        grad_end = decay_list[b][:, None, None] * grad_end + moments[b]
    shape_out = (tok_dev, head_dev * head_width)
    grad_queries = q_parts[0].reshape(shape_out).astype(jnp.bfloat16)
    grad_keys = k_parts[0].reshape(shape_out).astype(jnp.bfloat16)
    grad_values = v_parts[0].reshape(shape_out).astype(jnp.bfloat16)
    return (attn_out, grad_queries, grad_keys, grad_values, grad_gain)


def solution(mesh):
    placed = (
        P("ctx", "tp"),
        P("ctx", "tp"),
        P("ctx", "tp"),
        P("ctx", "tp"),
        P("tp"),
        P("ctx", "tp"),
    )
    return jax.shard_map(
        body,
        mesh=mesh,
        in_specs=placed,
        out_specs=(P("ctx", "tp"), P("ctx", "tp"), P("ctx", "tp"), P("ctx", "tp"), P("tp")),
        check_vma=False,
    )
```

profile of v0, /device:TPU:1, one launch (start us, length us, event | category | flops | bytes accessed | tf_op | source)
XLA Modules:
  0.0 437.4 jit_solution(16135141861203743281)
XLA Ops:
  8.0 1.2 reduce-window.6
  9.9 1.3 copy.109
  11.2 1.4 convolution_add_fusion
  12.7 39.7 %all-gather.2 = f32[64,1,4]{2,1,0:T(1,128)S(1)} all-gather(f32[1,1,4]{2,1,0:T(1,128)S(1)} %bitcast.155), channel_id=1, replica_groups=mesh['ctx'=64,'tp'=8] {'ctx'}, dimensions={0}, use_global_device_ids=true | all-gather | bytes 1040 | tf_op jit(solution)/shard_map/all_gather | solution.py:72
  52.6 1.3 copy.108
  54.7 1.3 multiply_convert_fusion.1
  56.0 1.3 copy-done.1
  58.2 65.4 %all-gather.7.cloned.1.call-done = f32[256,128,128]{2,1,0:T(8,128)} async-done(((f32[4,128,128]{2,1,0:T(8,128)}), f32[256,128,128]{2,1,0:T(8,128)}) %all-gather.7.cloned.1.call-update) | async-done | bytes 16777232 | tf_op jit(solution)/shard_map/all_gather | solution.py:78
  123.5 22.5 %fusion = f32[4,1,128,128]{3,1,2,0:T(1,128)S(1)} fusion(f32[64,4,1,1]{0,2,3,1:T(1,128)S(1)} %copy.132, f32[64,4,128,128]{3,2,1,0:T(8,128)} %bitcast.128), kind=kOutput, calls=%fused_computation.2 | convolution fusion | flops 50331648 | bytes 17040384 | tf_op jit(solution)/shard_map/nh,nhde->hde/dot_general | solution.py:83
  146.1 1.7 multiply_reduce_fusion
  147.8 14.4 %psum.21 = f32[512]{0:T(512)S(1)} all-reduce(f32[512]{0:T(512)S(1)} %get-tuple-element.137), channel_id=1, replica_groups=mesh['ctx'=64,'tp'=8] {'tp'}, use_global_device_ids=true, to_apply=%region_4.5 | all-reduce | flops 512 | bytes 4096 | tf_op jit(solution)/shard_map/psum | solution.py:95
  162.2 1.6 copy.116
  164.2 11.3 %psum.22 = f32[512]{0:T(512)S(1)} all-reduce(f32[512]{0:T(512)S(1)} %get-tuple-element.116), channel_id=1, replica_groups=mesh['ctx'=64,'tp'=8] {'tp'}, use_global_device_ids=true, to_apply=%region_6.7 | all-reduce | flops 512 | bytes 4096 | tf_op jit(solution)/shard_map/psum | solution.py:95
  175.5 1.1 fusion.16
  176.9 1.4 fusion.19
  178.3 41.1 %all-gather.3 = f32[64,1,4]{2,1,0:T(1,128)S(1)} all-gather(f32[1,1,4]{2,1,0:T(1,128)S(1)} %bitcast.156), channel_id=1, replica_groups=mesh['ctx'=64,'tp'=8] {'ctx'}, dimensions={0}, use_global_device_ids=true | all-gather | bytes 1040 | tf_op jit(solution)/shard_map/all_gather | solution.py:14
  219.4 2.3 multiply_convert_fusion
  221.7 1.3 copy-done.3
  223.0 2.0 convolution_bitcast_fusion.2
  225.0 2.5 fusion.10
  227.5 2.0 copy.127
  229.5 125.2 %psum.23 = f32[512]{0:T(512)} all-reduce(f32[512]{0:T(512)S(1)} %get-tuple-element.115), channel_id=1, replica_groups=mesh['ctx'=64,'tp'=8] {'ctx'}, use_global_device_ids=true, to_apply=%region_10.11 | all-reduce | flops 512 | bytes 4096 | tf_op jit(solution)/shard_map/psum | solution.py:101
  354.7 2.6 convolution_bitcast_fusion.1
  357.8 68.3 %while.14 = (s32[]{:T(128)}, f32[4,128,128]{2,1,0:T(8,128)S(1)}, s32[]{:T(128)}, f32[64,4]{1,0:T(8,128)S(1)}, f32[64,4,128,128]{3,2,1,0:T(8,128)}, /*index=5*/s32[]{:T(128)}, s32[]{:T(128)}, s32[]{:T(128)}, s32[]{:T(128)}) while((s32[]{:T(128)}, f32[4,128,128]{2,1,0:T(8,128)S(1)}, s32[]{:T(128)}, f32[64,4]{1,0:T(8,128)S(1)}, ...), condition=%wide.region_8.9_spmd, body=%wide.region_7.8_spmd.sunk | while | flops 131078 | bytes 786635 | solution.py:23
  357.9 1.1 bitcast_add_fusion.2
  360.1 1.1 bitcast_add_fusion.2
  362.3 1.1 bitcast_add_fusion.2
  363.4 1.1 bitcast_add_fusion.2
  365.6 1.1 bitcast_add_fusion.2
  366.7 1.1 bitcast_add_fusion.2
  368.9 1.1 bitcast_add_fusion.2
  371.1 1.1 bitcast_add_fusion.2
  372.2 1.1 bitcast_add_fusion.2
  374.4 1.1 bitcast_add_fusion.2
  375.5 1.1 bitcast_add_fusion.2
  377.7 1.1 bitcast_add_fusion.2
  378.8 1.1 bitcast_add_fusion.2
  381.0 1.1 bitcast_add_fusion.2
  383.2 1.1 bitcast_add_fusion.2
  384.3 1.1 bitcast_add_fusion.2
  386.5 1.1 bitcast_add_fusion.2
  387.6 1.1 bitcast_add_fusion.2
  389.8 1.1 bitcast_add_fusion.2
  392.0 1.1 bitcast_add_fusion.2
  393.1 1.1 bitcast_add_fusion.2
  395.3 1.1 bitcast_add_fusion.2
  396.4 1.1 bitcast_add_fusion.2
  398.6 1.1 bitcast_add_fusion.2
  399.7 1.1 bitcast_add_fusion.2
  401.9 1.1 bitcast_add_fusion.2
  404.1 1.1 bitcast_add_fusion.2
  405.2 1.1 bitcast_add_fusion.2
  407.4 1.1 bitcast_add_fusion.2
  408.5 1.1 bitcast_add_fusion.2
  410.7 1.1 bitcast_add_fusion.2
  412.9 1.1 bitcast_add_fusion.2
  414.0 1.1 bitcast_add_fusion.2
  416.2 1.1 bitcast_add_fusion.2
  417.3 1.1 bitcast_add_fusion.2
  419.5 1.1 bitcast_add_fusion.2
  420.6 1.1 bitcast_add_fusion.2
  422.8 1.1 bitcast_add_fusion.2
  425.0 1.1 bitcast_add_fusion.2
  426.1 1.9 fusion.12
  (134 shorter events, 32.2 us)
Async XLA Ops:
  7.2 4.0 copy-start
  7.2 116.3 %all-gather.7.cloned.1.call-start = ((), (), s32[]{:S(2)}) async-start(), calls=%async_computation | async-start | bytes 17039360 | tf_op jit(solution)/shard_map/all_gather | solution.py:78
  11.2 44.8 %copy-start.6 = (bf16[512,512]{0,1:T(8,128)(2,1)}, bf16[512,512]{0,1:T(8,128)(2,1)S(1)}, u32[]{:S(2)}) copy-start(bf16[512,512]{0,1:T(8,128)(2,1)S(1)} %copy.109) | copy-start | bytes 1572868
  12.6 345.2 %all-gather.9.cloned.1.call-start = ((), (), s32[]{:S(2)}) async-start(), calls=%async_computation.1 | async-start | bytes 17039360 | tf_op jit(solution)/shard_map/all_gather | solution.py:14
  54.0 0.7 copy-start.9
  56.0 1.4 copy-start.1
  146.1 17.7 %copy-start.8 = (bf16[512,512]{1,0:T(8,128)(2,1)S(1)}, bf16[512,512]{1,0:T(8,128)(2,1)}, u32[]{:S(2)}) copy-start(bf16[512,512]{1,0:T(8,128)(2,1)} %param.13) | copy-start | bytes 1572868
  146.1 17.7 %copy-start.10 = (f32[512]{0:T(512)S(1)}, f32[512]{0:T(512)}, u32[]{:S(2)}) copy-start(f32[512]{0:T(512)} %param.12) | copy-start | bytes 6148
  176.9 42.5 %copy-start.5 = (bf16[512,512]{0,1:T(8,128)(2,1)}, bf16[512,512]{0,1:T(8,128)(2,1)S(1)}, u32[]{:S(2)}) copy-start(bf16[512,512]{0,1:T(8,128)(2,1)S(1)} %copy.139) | copy-start | bytes 1572868
  221.7 1.3 copy-start.3
  223.0 131.7 %copy-start.2 = (bf16[4,512,512]{2,1,0:T(8,128)(2,1)S(1)}, bf16[4,512,512]{2,1,0:T(8,128)(2,1)}, u32[]{:S(2)}) copy-start(bf16[4,512,512]{2,1,0:T(8,128)(2,1)} %copy-done.1) | copy-start | bytes 6291460
  354.7 2.6 copy-start.4
  357.3 68.8 %copy-start.7 = (bf16[512,512]{0,1:T(8,128)(2,1)S(1)}, bf16[512,512]{0,1:T(8,128)(2,1)}, u32[]{:S(2)}) copy-start(bf16[512,512]{0,1:T(8,128)(2,1)} %copy-done.6) | copy-start | bytes 1572868
Sparse Core Ops, SparseCore 0:
  12.7 110.7 all-gather.6
  178.4 107.4 all-gather.8
where the time goes:
time: 443 us; the launch traced here: 437 us
  blocking collectives  232 us (52%)
  other arithmetic  69.2 us (16%)
  waiting for transfers between devices  65.4 us (15%)
  matrix products  41.4 us (9%)
  between operations  14.3 us (3%)
  local copies, waits for them, and re-layouts  13.5 us (3%)
    psum x1, blocking collectives, body(): grad_gain = lax.psum(jnp.sum(normed * up_grad, axis=0), 'ctx')  125 us
    add x62, other arithmetic, chain_link(): later[0][:, None, None] * earlier[1] + later[1]  65.8 us
    all_gather x1, waiting for transfers between devices, body(): piece = lax.all_gather(total_state[None], 'ctx', axis=0, tiled=True)  65.4 us
    all_gather x1, blocking collectives, entering_2(): gathered = jax.tree.map(lambda a: lax.all_gather(a, axis), part)  41.1 us
    all_gather x1, blocking collectives, body(): all_logs = lax.all_gather(log_total[None, :], 'ctx', axis=0, tiled=True)  39.7 us
    psum x2, blocking collectives, body(): lax.psum((jnp.sum(attended * attended, axis=1), jnp.sum(attended * scaled...  25.7 us
    dot_general x1, matrix products, body(): incoming = jnp.einsum('nh,nhde->hde', factor, piece, precision=highest)  22.5 us
    unnamed x28, local copies, waits for them, and re-layouts  9.96 us
  transfers between devices with their start and end apart: 2, of which 1 were waited for; matrix products, arithmetic and copies ran while one was open for 4% of the time, Pallas kernels for 0%

commit v1 on v0

v1 whole, which is shorter than its diff:
```python
import functools

import jax
import jax.numpy as jnp
from jax import lax
from jax.experimental import pallas as pl
from jax.experimental.pallas import tpu as pltpu
from jax.sharding import PartitionSpec as P

MESH = pl.DeviceIdType.MESH
FEAT = 4096
BLK = 512
DH = 128
HEADS = 4
ROWB = 128
NRB = BLK // ROWB
CHIPS = 8
GROUPS = 4
TP = 8
SLICE = 2 * DH // CHIPS
F32 = jnp.float32
BF16 = jnp.bfloat16


def mm(a, b, ca, cb):
    return lax.dot_general(a, b, (((ca,), (cb,)), ((), ())), preferred_element_type=F32)


def split(x):
    hi = x.astype(BF16)
    return hi, (x - hi.astype(F32)).astype(BF16)


def bcast_col(row):
    return jnp.broadcast_to(row, (ROWB, row.shape[1])).T


class Scan:
    def __init__(self, refs, place):
        (
            self.out0, self.in0, self.out1, self.in1, self.out2, self.in2, self.out3, self.in3, self.out4, self.in4,
            self.s0, self.r0, self.s1, self.r1, self.s2, self.r2, self.s3, self.r3, self.s4, self.r4,
        ) = refs
        self.core, self.p, self.g, self.tp = place

    def device(self, g, p, core):
        return ((g * CHIPS + p) * 2 + core, self.tp)

    def core_copy(self, src, dst, send, recv):
        return pltpu.make_async_remote_copy(
            src_ref=src, dst_ref=dst, send_sem=send.at[0], recv_sem=recv.at[0],
            device_id=self.device(self.g, self.p, 1 - self.core), device_id_type=MESH,
        )

    def copy0(self):
        return self.core_copy(self.out0, self.in0, self.s0, self.r0)

    def copy4(self):
        return self.core_copy(self.out4, self.in4, self.s4, self.r4)

    def group_copy(self, d, src, dst, send, recv, arriving):
        peer = (self.p + d) % CHIPS
        slot = peer if arriving else self.p
        return pltpu.make_async_remote_copy(
            src_ref=src.at[peer], dst_ref=dst.at[slot], send_sem=send.at[d], recv_sem=recv.at[slot],
            device_id=self.device(self.g, peer, self.core), device_id_type=MESH,
        )

    def copy1(self, d, arriving=False):
        return self.group_copy(d, self.out1, self.in1, self.s1, self.r1, arriving)

    def copy3(self, d, arriving=False):
        return self.group_copy(d, self.out3, self.in3, self.s3, self.r3, arriving)

    def copy2(self, d, arriving=False):
        peer = (self.g + d) % GROUPS
        slot = peer if arriving else self.g
        return pltpu.make_async_remote_copy(
            src_ref=self.out2, dst_ref=self.in2.at[slot], send_sem=self.s2.at[d], recv_sem=self.r2.at[slot],
            device_id=self.device(peer, self.p, self.core), device_id_type=MESH,
        )


GROUP_ORDER = (6, 2, 4, 5, 3, 7, 1)
RING_ORDER = (2, 1, 3)
TP_ORDER = (4, 3, 5, 2, 6, 1, 7)


def kernel(*refs):
    (q_ref, k_ref, v_ref, log_ref, gain_ref, u_ref, out_ref, gq_ref, gk_ref, gv_ref, gg_ref) = refs[:11]
    (
        crow, rise, fall, dec, w_st, p_st, g_st, a_st, su_st, da_st, gk_st, gv_st, own_st, s_st, r_st, ggp,
        zout, zin, zs, zr,
    ) = refs[11:31]
    ctx = lax.axis_index("ctx")
    tp = lax.axis_index("tp")
    core = ctx % 2
    chip = ctx // 2
    p = chip % CHIPS
    g = chip // CHIPS
    place = (core, p, g, tp)
    fwd = Scan(refs[31:51], place)
    bwd = Scan(refs[51:71], place)
    first = core == 0

    def tp_copy(d, arriving=False):
        peer = (tp + d) % TP
        slot = peer if arriving else tp
        return pltpu.make_async_remote_copy(
            src_ref=zout, dst_ref=zin.at[slot], send_sem=zs.at[d], recv_sem=zr.at[slot],
            device_id=(ctx, peer), device_id_type=MESH,
        )

    barrier = pltpu.get_barrier_semaphore()
    partners = [fwd.device(g, p, 1 - core)]
    partners += [fwd.device(g, (p + d) % CHIPS, core) for d in range(1, CHIPS)]
    partners += [fwd.device((g + d) % GROUPS, p, core) for d in range(1, GROUPS)]
    partners += [(ctx, (tp + d) % TP) for d in range(1, TP)]
    for partner in partners:
        pl.semaphore_signal(barrier, inc=1, device_id=partner, device_id_type=MESH)

    cum = log_ref[...]
    lane = lax.broadcasted_iota(jnp.int32, cum.shape, 1)
    step = 1
    while step < BLK:
        cum = cum + jnp.where(lane >= step, pltpu.roll(cum, step, axis=1), 0.0)
        step *= 2
    for h in range(HEADS):
        row = cum[h : h + 1, :]
        crow[h] = row
        last = jnp.broadcast_to(row[:, BLK - 1 : BLK], (1, DH))
        dec[h] = jnp.exp(last)
        for rb in range(NRB):
            rows = slice(rb * ROWB, (rb + 1) * ROWB)
            col = bcast_col(row[:, rows])
            rise[h, rows, :] = col
            fall[h, rows, :] = jnp.exp(last - col)

    def lanes(h):
        if isinstance(h, int):
            return slice(h * DH, (h + 1) * DH)
        return pl.ds(pl.multiple_of(h * DH, DH), DH)

    def keyed_state(h):
        total = None
        for rb in range(NRB):
            rows = slice(rb * ROWB, (rb + 1) * ROWB)
            hi, lo = split(k_ref[rows, lanes(h)].astype(F32) * fall[h, rows, :])
            vv = v_ref[rows, lanes(h)]
            term = mm(hi, vv, 0, 0) + mm(lo, vv, 0, 0)
            total = term if total is None else total + term
        return total

    def moment(h):
        total = None
        for rb in range(NRB):
            rows = slice(rb * ROWB, (rb + 1) * ROWB)
            hi, lo = split(q_ref[rows, lanes(h)].astype(F32) * jnp.exp(rise[h, rows, :]))
            dd = da_st[rows, lanes(h)]
            term = mm(hi, dd, 0, 0) + mm(lo, dd, 0, 0)
            total = term if total is None else total + term
        return total

    mine = 2 * core
    other = 2 * (1 - core)
    for j in range(2):
        fwd.out0[j * DH : (j + 1) * DH, :] = keyed_state(other + j)
        fwd.out0[2 * DH + j : 2 * DH + j + 1, :] = dec[other + j]
    fwd.out0[2 * DH + 2 : 2 * DH + 8, :] = jnp.zeros((6, DH), F32)
    pl.semaphore_wait(barrier, len(partners))
    fwd.copy0().start()
    for j in range(2):
        own_st[j] = keyed_state(mine + j)

    def send_chip(scan, backward):
        scan.copy0().wait()
        for j in range(2):
            theirs = scan.in0[j * DH : (j + 1) * DH, :]
            ours = own_st[j]
            d_ours, d_theirs = dec[mine + j], fwd.in0[2 * DH + j : 2 * DH + j + 1, :]
            if backward:
                chip_state = jnp.where(first, d_ours * theirs + ours, d_theirs * ours + theirs)
                tail = scan.in0[2 * DH : 2 * DH + 8, :] + scan.out0[2 * DH : 2 * DH + 8, :]
            else:
                chip_state = jnp.where(first, d_theirs * ours + theirs, d_ours * theirs + ours)
                tail = jnp.broadcast_to(d_ours * d_theirs, (8, DH))
            for piece in range(CHIPS // 2):
                slot = j * (CHIPS // 2) + piece
                scan.out1[slot, 0:SLICE, :] = chip_state[piece * SLICE : (piece + 1) * SLICE, :]
                scan.out1[slot, SLICE : SLICE + 8, :] = tail
        for d in GROUP_ORDER:
            scan.copy1(d).start()
        scan.in1[p] = scan.out1[p]

    def send_group(scan, backward):
        for d in range(1, CHIPS):
            scan.copy1(d, True).wait_recv()
        total = jnp.zeros((SLICE, DH), F32)
        tail = jnp.zeros((8, DH), F32) if backward else jnp.ones((8, DH), F32)
        for s in range(CHIPS):
            at = CHIPS - 1 - s if backward else s
            total = fwd.in1[at, SLICE : SLICE + 1, :] * total + scan.in1[at, 0:SLICE, :]
            if backward:
                tail = tail + scan.in1[s, SLICE : SLICE + 8, :]
            else:
                tail = tail * scan.in1[s, SLICE : SLICE + 8, :]
        scan.out2[0:SLICE, :] = total
        scan.out2[SLICE : SLICE + 8, :] = tail
        for d in RING_ORDER:
            scan.copy2(d).start()
        scan.in2[g] = scan.out2[...]

    def send_back(scan, backward):
        for d in range(1, GROUPS):
            scan.copy2(d, True).wait_recv()
        state = jnp.zeros((SLICE, DH), F32)
        for s in range(GROUPS):
            at = GROUPS - 1 - s if backward else s
            later = fwd.in2[at, SLICE : SLICE + 1, :] * state + scan.in2[at, 0:SLICE, :]
            state = jnp.where(at > g if backward else at < g, later, state)
        for s in range(CHIPS):
            at = CHIPS - 1 - s if backward else s
            scan.out3[at] = state
            state = fwd.in1[at, SLICE : SLICE + 1, :] * state + scan.in1[at, 0:SLICE, :]
        for d in GROUP_ORDER:
            scan.copy3(d).start()
        scan.in3[p] = scan.out3[p]

    def receive(scan, backward, store):
        for d in range(1, CHIPS):
            scan.copy3(d, True).wait_recv()
        for j in range(2):
            half = CHIPS // 2
            entering = scan.in3[j * half : (j + 1) * half].reshape(DH, DH)
            theirs = scan.in0[j * DH : (j + 1) * DH, :]
            ours = own_st[j]
            d_ours, d_theirs = dec[mine + j], fwd.in0[2 * DH + j : 2 * DH + j + 1, :]
            past_ours = d_ours * entering + ours
            past_theirs = d_theirs * entering + theirs
            far = jnp.logical_not(first) if not backward else first
            store[mine + j] = jnp.where(far, past_theirs, entering)
            scan.out4[j] = jnp.where(far, entering, past_ours)
        scan.copy4().start()

    def intra_forward(h):
        for rb in range(NRB):
            rows = slice(rb * ROWB, (rb + 1) * ROWB)
            wide = (rb + 1) * ROWB
            raw = mm(q_ref[rows, lanes(h)], k_ref[0:wide, lanes(h)], 1, 1)
            col = rise[h, rows, :]
            for cb in range(rb + 1):
                cols = slice(cb * ROWB, (cb + 1) * ROWB)
                diff = col - crow[h, :, cols]
                if cb == rb:
                    i = lax.broadcasted_iota(jnp.int32, (ROWB, ROWB), 0)
                    j = lax.broadcasted_iota(jnp.int32, (ROWB, ROWB), 1)
                    diff = jnp.where(i >= j, diff, -jnp.inf)
                weight = jnp.exp(diff)
                w_st[h, rows, cols] = weight
                p_st[h, rows, cols] = (raw[:, cols] * weight).astype(BF16)
            a_st[rows, lanes(h)] = mm(p_st[h, rows, 0:wide], v_ref[0:wide, lanes(h)], 1, 0)

    def scale_upstream(h):
        su_st[:, lanes(h)] = u_ref[:, lanes(h)].astype(F32) * gain_ref[:, lanes(h)]

    def outer(h):
        hi, lo = split(s_st[h])
        for rb in range(NRB):
            rows = slice(rb * ROWB, (rb + 1) * ROWB)
            qq = q_ref[rows, lanes(h)]
            a_st[rows, lanes(h)] += jnp.exp(rise[h, rows, :]) * (mm(qq, hi, 1, 0) + mm(qq, lo, 1, 0))

    def intra_backward(h):
        hi, lo = split(s_st[h])
        for rb in range(NRB):
            rows = slice(rb * ROWB, (rb + 1) * ROWB)
            wide = (rb + 1) * ROWB
            dd = da_st[rows, lanes(h)]
            raw = mm(dd, v_ref[0:wide, lanes(h)], 1, 1)
            for cb in range(rb + 1):
                cols = slice(cb * ROWB, (cb + 1) * ROWB)
                g_st[rows, cols] = (raw[:, cols] * w_st[h, rows, cols]).astype(BF16)
            inner = mm(g_st[rows, 0:wide], k_ref[0:wide, lanes(h)], 1, 0)
            cross = mm(dd, hi, 1, 1) + mm(dd, lo, 1, 1)
            gq_ref[rows, lanes(h)] = (inner + jnp.exp(rise[h, rows, :]) * cross).astype(BF16)
        for cb in range(NRB):
            cols = slice(cb * ROWB, (cb + 1) * ROWB)
            below = slice(cb * ROWB, BLK)
            gk_st[cols, lanes(h)] = mm(g_st[below, cols], q_ref[below, lanes(h)], 0, 0)
            gv_st[cols, lanes(h)] = mm(p_st[h, below, cols], da_st[below, lanes(h)], 0, 0)

    def finish(h):
        hi, lo = split(r_st[h])
        for rb in range(NRB):
            rows = slice(rb * ROWB, (rb + 1) * ROWB)
            vv, kk, down = v_ref[rows, lanes(h)], k_ref[rows, lanes(h)], fall[h, rows, :]
            gk_ref[rows, lanes(h)] = (
                gk_st[rows, lanes(h)] + down * (mm(vv, hi, 1, 1) + mm(vv, lo, 1, 1))
            ).astype(BF16)
            gv_ref[rows, lanes(h)] = (
                gv_st[rows, lanes(h)] + down * (mm(kk, hi, 1, 0) + mm(kk, lo, 1, 0))
            ).astype(BF16)

    send_chip(fwd, False)
    intra_forward(0)
    intra_forward(1)
    send_group(fwd, False)
    intra_forward(2)
    intra_forward(3)
    send_back(fwd, False)
    for h in range(HEADS):
        scale_upstream(h)
    receive(fwd, False, s_st)
    for j in range(2):
        outer(mine + j)
    fwd.copy4().wait()
    for j in range(2):
        s_st[other + j] = fwd.in4[j]
        outer(other + j)

    for rb in range(NRB):
        rows = slice(rb * ROWB, (rb + 1) * ROWB)
        squares = jnp.zeros((ROWB, DH), F32)
        crosses = jnp.zeros((ROWB, DH), F32)
        for h in range(HEADS):
            act = a_st[rows, lanes(h)]
            squares = squares + act * act
            crosses = crosses + act * su_st[rows, lanes(h)]
        zout[rb : rb + 1, :] = jnp.sum(squares.T, axis=0, keepdims=True)
        zout[NRB + rb : NRB + rb + 1, :] = jnp.sum(crosses.T, axis=0, keepdims=True)
    for d in TP_ORDER:
        tp_copy(d).start()
    zin[tp] = zout[...]
    for d in range(1, TP):
        tp_copy(d, True).wait_recv()
    sums = zin[0]
    for s in range(1, TP):
        sums = sums + zin[s]
    inv_rms = lax.rsqrt(sums[0:NRB, :] / FEAT + 1e-06)
    pull = inv_rms * inv_rms * inv_rms * (sums[NRB : 2 * NRB, :] / FEAT)
    gain_terms = [jnp.zeros((1, DH), F32)] * HEADS
    for rb in range(NRB):
        rows = slice(rb * ROWB, (rb + 1) * ROWB)
        scale = bcast_col(inv_rms[rb : rb + 1, :])
        back = bcast_col(pull[rb : rb + 1, :])
        for h in range(HEADS):
            act = a_st[rows, lanes(h)]
            normed = act * scale
            out_ref[rows, lanes(h)] = (normed * gain_ref[:, lanes(h)]).astype(BF16)
            da_st[rows, lanes(h)] = (scale * su_st[rows, lanes(h)] - act * back).astype(BF16)
            gain_terms[h] = gain_terms[h] + jnp.sum(
                normed * u_ref[rows, lanes(h)].astype(F32), axis=0, keepdims=True
            )
    for h in range(HEADS):
        bwd.out0[2 * DH + h : 2 * DH + h + 1, :] = gain_terms[h]
    bwd.out0[2 * DH + 4 : 2 * DH + 8, :] = jnp.zeros((4, DH), F32)
    for j in range(2):
        bwd.out0[j * DH : (j + 1) * DH, :] = moment(other + j)
    bwd.copy0().start()
    for j in range(2):
        own_st[j] = moment(mine + j)
    send_chip(bwd, True)
    intra_backward(0)
    intra_backward(1)
    send_group(bwd, True)
    intra_backward(2)
    intra_backward(3)
    send_back(bwd, True)
    gain_sum = bwd.in2[0, SLICE : SLICE + 8, :]
    for s in range(1, GROUPS):
        gain_sum = gain_sum + bwd.in2[s, SLICE : SLICE + 8, :]
    for h in range(HEADS):
        gg_ref[:, lanes(h)] = gain_sum[h : h + 1, :]
    receive(bwd, True, r_st)
    for j in range(2):
        finish(mine + j)
    bwd.copy4().wait()
    for j in range(2):
        r_st[other + j] = bwd.in4[j]
        finish(other + j)

    for scan in (fwd, bwd):
        for d in range(1, CHIPS):
            scan.copy1(d).wait_send()
            scan.copy3(d).wait_send()
        for d in range(1, GROUPS):
            scan.copy2(d).wait_send()
    for d in range(1, TP):
        tp_copy(d).wait_send()


def scan_scratch():
    dma = pltpu.SemaphoreType.DMA
    wide = SLICE + 8
    return [
        pltpu.VMEM((2 * DH + 8, DH), F32),
        pltpu.VMEM((2 * DH + 8, DH), F32),
        pltpu.VMEM((CHIPS, wide, DH), F32),
        pltpu.VMEM((CHIPS, wide, DH), F32),
        pltpu.VMEM((wide, DH), F32),
        pltpu.VMEM((GROUPS, wide, DH), F32),
        pltpu.VMEM((CHIPS, SLICE, DH), F32),
        pltpu.VMEM((CHIPS, SLICE, DH), F32),
        pltpu.VMEM((2, DH, DH), F32),
        pltpu.VMEM((2, DH, DH), F32),
        dma((1,)), dma((1,)), dma((CHIPS,)), dma((CHIPS,)), dma((GROUPS,)),
        dma((GROUPS,)), dma((CHIPS,)), dma((CHIPS,)), dma((1,)), dma((1,)),
    ]


def body(queries, keys, values, log_decay, gain, upstream):
    vmem = pl.BlockSpec(memory_space=pltpu.VMEM)
    big = jax.ShapeDtypeStruct((BLK, HEADS * DH), BF16)
    dma = pltpu.SemaphoreType.DMA
    scratch = [
        pltpu.VMEM((HEADS, 1, BLK), F32),
        pltpu.VMEM((HEADS, BLK, DH), F32),
        pltpu.VMEM((HEADS, BLK, DH), F32),
        pltpu.VMEM((HEADS, 1, DH), F32),
        pltpu.VMEM((HEADS, BLK, BLK), F32),
        pltpu.VMEM((HEADS, BLK, BLK), BF16),
        pltpu.VMEM((BLK, BLK), BF16),
        pltpu.VMEM((BLK, HEADS * DH), F32),
        pltpu.VMEM((BLK, HEADS * DH), F32),
        pltpu.VMEM((BLK, HEADS * DH), BF16),
        pltpu.VMEM((BLK, HEADS * DH), F32),
        pltpu.VMEM((BLK, HEADS * DH), F32),
        pltpu.VMEM((2, DH, DH), F32),
        pltpu.VMEM((HEADS, DH, DH), F32),
        pltpu.VMEM((HEADS, DH, DH), F32),
        pltpu.VMEM((8, DH), F32),
        pltpu.VMEM((8, DH), F32),
        pltpu.VMEM((TP, 8, DH), F32),
        dma((TP,)),
        dma((TP,)),
    ]
    attn, gq, gk, gv, gg = pl.pallas_call(
        kernel,
        out_shape=(big, big, big, big, jax.ShapeDtypeStruct((1, HEADS * DH), F32)),
        in_specs=[vmem] * 6,
        out_specs=(vmem,) * 5,
        scratch_shapes=scratch + scan_scratch() + scan_scratch(),
        compiler_params=pltpu.CompilerParams(
            collective_id=0, has_side_effects=True, vmem_limit_bytes=40 * 2**20
        ),
        name="attention",
    )(queries, keys, values, log_decay.T, gain.reshape(1, HEADS * DH), upstream)
    return attn, gq, gk, gv, gg.reshape(HEADS * DH)


def solution(mesh):
    placed = (P("ctx", "tp"),) * 4 + (P("tp"), P("ctx", "tp"))
    return jax.shard_map(
        body,
        mesh=mesh,
        in_specs=placed,
        out_specs=(P("ctx", "tp"),) * 4 + (P("tp"),),
        check_vma=False,
    )
```

time: 443 us -> 65.1 us (0.15); the launches traced: 437 us -> 64.8 us
  blocking collectives: 232 us -> 0 us
  other arithmetic: 69.2 us -> 0 us
  waiting for transfers between devices: 65.4 us -> 0 us
  Pallas kernels: 0 us -> 54.8 us
  matrix products: 41.4 us -> 0 us
  between operations: 14.3 us -> 0.66 us
    psum x3 -> x0, blocking collectives: 151 us -> none  [the longest x1 125 us: body(): grad_gain = lax.psum(jnp.sum(normed * up_grad, axis=0), 'ctx')]
    all_gather x2 -> x0, blocking collectives: 80.8 us -> none  [the longest x1 41.1 us: entering_2(): gathered = jax.tree.map(lambda a: lax.all_gather(a, axis), part)]
    add x62 -> x0, other arithmetic: 65.8 us -> none  [chain_link(): later[0][:, None, None] * earlier[1] + later[1]]
    all_gather x2 -> x0, waiting for transfers between devices: 65.4 us -> none  [the longest x1 65.4 us: body(): piece = lax.all_gather(total_state[None], 'ctx', axis=0, tiled=True)]
    pallas_call x0 -> x1, Pallas kernels: none -> 54.8 us  [body(): pl.pallas_call(kernel, out_shape=(big, big, big, big, jax.ShapeDtypeStruc...]
    dot_general x13 -> x0, matrix products: 41.4 us -> none  [the longest x1 22.5 us: body(): incoming = jnp.einsum('nh,nhde->hde', factor, piece, precision=highest)]
    unnamed x28 -> x17, local copies, waits for them, and re-layouts: 9.96 us -> 9.29 us
  transfers between devices with their start and end apart: 2 -> 0, of which waited for: 1 -> 0; matrix products, arithmetic and copies ran while one was open for 4% -> 0% of each run, Pallas kernels for 0% -> 0%
where the time goes in v1:
time: 65.1 us; the launch traced here: 64.8 us
  Pallas kernels  54.8 us (84%)
  local copies, waits for them, and re-layouts  9.29 us (14%)
  between operations  0.66 us (1%)
    pallas_call x1, Pallas kernels, body(): pl.pallas_call(kernel, out_shape=(big, big, big, big, jax.ShapeDtypeStruc...  54.8 us
    unnamed x17, local copies, waits for them, and re-layouts  9.29 us

profile of v1, /device:TPU:1, one launch (start us, length us, event | category | flops | bytes accessed | tf_op | source)
XLA Modules:
  0.0 64.8 jit_solution(4096161245400828450)
XLA Ops:
  0.6 0.0 copy-start.5
  0.6 0.7 %copy-done.5 = f32[512]{0:T(512)S(1)} copy-done((f32[512]{0:T(512)S(1)}, f32[512]{0:T(512)}, u32[]{:S(2)}) %copy-start.5) | copy-done | bytes 2072
  1.3 0.0 copy-start
  1.3 1.0 %copy-done = bf16[512,512]{1,0:T(8,128)(2,1)S(1)} copy-done((bf16[512,512]{1,0:T(8,128)(2,1)S(1)}, bf16[512,512]{1,0:T(8,128)(2,1)}, u32[]{:S(2)}) %copy-start) | copy-done | bytes 524312
  2.4 0.0 copy-start.1
  2.4 1.0 %copy-done.1 = bf16[512,512]{1,0:T(8,128)(2,1)S(1)} copy-done((bf16[512,512]{1,0:T(8,128)(2,1)S(1)}, bf16[512,512]{1,0:T(8,128)(2,1)}, u32[]{:S(2)}) %copy-start.1) | copy-done | bytes 524312
  3.4 0.0 copy-start.2
  3.4 1.0 %copy-done.2 = bf16[512,512]{1,0:T(8,128)(2,1)S(1)} copy-done((bf16[512,512]{1,0:T(8,128)(2,1)S(1)}, bf16[512,512]{1,0:T(8,128)(2,1)}, u32[]{:S(2)}) %copy-start.2) | copy-done | bytes 524312
  4.4 0.0 copy-start.3
  4.4 1.0 %copy-done.3 = bf16[512,512]{1,0:T(8,128)(2,1)S(1)} copy-done((bf16[512,512]{1,0:T(8,128)(2,1)S(1)}, bf16[512,512]{1,0:T(8,128)(2,1)}, u32[]{:S(2)}) %copy-start.3) | copy-done | bytes 524312
  5.5 0.0 copy-start.4
  5.5 0.7 %copy-done.4 = f32[512,4]{0,1:T(4,128)S(1)} copy-done((f32[512,4]{0,1:T(4,128)S(1)}, f32[512,4]{0,1:T(4,128)}, u32[]{:S(2)}) %copy-start.4) | copy-done | bytes 8216
  6.2 54.8 %attention.1 = (bf16[512,512]{1,0:T(8,128)(2,1)S(1)}, bf16[512,512]{1,0:T(8,128)(2,1)S(1)}, bf16[512,512]{1,0:T(8,128)(2,1)S(1)}, bf16[512,512]{1,0:T(8,128)(2,1)S(1)}, f32[1,512]{1,0:T(1,128)S(1)}) custom-call(bf16[512,512]{1,0:T(8,128)(2,1)S(1)} %copy-done, bf16[512,512]{1,0:T(8,128)(2,1)S(1)} %copy-done.1, bf16[512,512]{1,0:T(8,128)(2,1)S(1)} %copy-done.2, ...), custom_call_target="tpu_custom_call" | custom-call | tf_op jit(solution)/shard_map/attention/pallas_call | solution.py:437
  61.0 0.8 %copy.16 = bf16[512,512]{1,0:T(8,128)(2,1)} copy(bf16[512,512]{1,0:T(8,128)(2,1)S(1)} %get-tuple-element.20) | data formatting | bytes 1048576
  61.8 0.8 %copy.17 = bf16[512,512]{1,0:T(8,128)(2,1)} copy(bf16[512,512]{1,0:T(8,128)(2,1)S(1)} %get-tuple-element.21) | data formatting | bytes 1048576
  62.6 0.8 %copy.18 = bf16[512,512]{1,0:T(8,128)(2,1)} copy(bf16[512,512]{1,0:T(8,128)(2,1)S(1)} %get-tuple-element.22) | data formatting | bytes 1048576
  63.4 0.8 %copy.19 = bf16[512,512]{1,0:T(8,128)(2,1)} copy(bf16[512,512]{1,0:T(8,128)(2,1)S(1)} %get-tuple-element.23) | data formatting | bytes 1048576
  64.2 0.6 copy.20
Async XLA Ops:
  0.6 0.7 %copy-start.5 = (f32[512]{0:T(512)S(1)}, f32[512]{0:T(512)}, u32[]{:S(2)}) copy-start(f32[512]{0:T(512)} %param.10) | copy-start | bytes 6148
  1.3 1.0 %copy-start = (bf16[512,512]{1,0:T(8,128)(2,1)S(1)}, bf16[512,512]{1,0:T(8,128)(2,1)}, u32[]{:S(2)}) copy-start(bf16[512,512]{1,0:T(8,128)(2,1)} %refs_0_.1) | copy-start | bytes 1572868
  2.4 1.0 %copy-start.1 = (bf16[512,512]{1,0:T(8,128)(2,1)S(1)}, bf16[512,512]{1,0:T(8,128)(2,1)}, u32[]{:S(2)}) copy-start(bf16[512,512]{1,0:T(8,128)(2,1)} %refs_1_.1) | copy-start | bytes 1572868
  3.4 1.0 %copy-start.2 = (bf16[512,512]{1,0:T(8,128)(2,1)S(1)}, bf16[512,512]{1,0:T(8,128)(2,1)}, u32[]{:S(2)}) copy-start(bf16[512,512]{1,0:T(8,128)(2,1)} %refs_2_.1) | copy-start | bytes 1572868
  4.4 1.0 %copy-start.3 = (bf16[512,512]{1,0:T(8,128)(2,1)S(1)}, bf16[512,512]{1,0:T(8,128)(2,1)}, u32[]{:S(2)}) copy-start(bf16[512,512]{1,0:T(8,128)(2,1)} %refs_5_.1) | copy-start | bytes 1572868
  5.5 0.7 %copy-start.4 = (f32[512,4]{0,1:T(4,128)S(1)}, f32[512,4]{0,1:T(4,128)}, u32[]{:S(2)}) copy-start(f32[512,4]{0,1:T(4,128)} %param.9) | copy-start | bytes 24580

commit v2 on v1

--- a/solution.py
+++ b/solution.py
@@ -86,12 +86,56 @@
 TP_ORDER = (4, 3, 5, 2, 6, 1, 7)
 
 
+def finish_head(columns, state, fall, v_ref, k_ref, gk_st, gv_st, gk_ref, gv_ref):
+    hi, lo = split(state)
+    for rb in range(NRB):
+        rows = slice(rb * ROWB, (rb + 1) * ROWB)
+        vv, kk, down = v_ref[rows, columns], k_ref[rows, columns], fall[rows, :]
+        gk_ref[rows, columns] = (
+            gk_st[rows, columns] + down * (mm(vv, hi, 1, 1) + mm(vv, lo, 1, 1))
+        ).astype(BF16)
+        gv_ref[rows, columns] = (
+            gv_st[rows, columns] + down * (mm(kk, hi, 1, 0) + mm(kk, lo, 1, 0))
+        ).astype(BF16)
+
+
+def tail_kernel(
+    out_in, gq_in, gk_in, gv_in, gg_in, gk_st, gv_st, r_st, fall, k_ref, v_ref,
+    out_hbm, gq_hbm, gk_hbm, gv_hbm, gg_hbm, gk_ref, gv_ref, sem,
+):
+    core = lax.axis_index("ctx") % 2
+
+    def half_store(src, dst, which, at):
+        columns = pl.ds(pl.multiple_of(which * 2 * DH, 2 * DH), 2 * DH)
+        return pltpu.make_async_copy(src.at[:, columns], dst.at[:, columns], sem.at[at])
+
+    stores = [
+        pltpu.make_async_copy(out_in, out_hbm, sem.at[0]),
+        pltpu.make_async_copy(gq_in, gq_hbm, sem.at[1]),
+        pltpu.make_async_copy(gg_in, gg_hbm, sem.at[2]),
+        half_store(gk_in, gk_hbm, core, 3),
+        half_store(gv_in, gv_hbm, core, 4),
+    ]
+    for store in stores:
+        store.start()
+    for j in range(2):
+        h = 2 * (1 - core) + j
+        columns = pl.ds(pl.multiple_of(h * DH, DH), DH)
+        finish_head(columns, r_st[h], fall.at[h], v_ref, k_ref, gk_st, gv_st, gk_ref, gv_ref)
+    last = [half_store(gk_ref, gk_hbm, 1 - core, 5), half_store(gv_ref, gv_hbm, 1 - core, 6)]
+    for store in last:
+        store.start()
+    for store in stores + last:
+        store.wait()
+
+
 def kernel(*refs):
-    (q_ref, k_ref, v_ref, log_ref, gain_ref, u_ref, out_ref, gq_ref, gk_ref, gv_ref, gg_ref) = refs[:11]
+    (q_hbm, k_hbm, v_hbm, log_hbm, gain_hbm, u_hbm) = refs[:6]
+    (out_ref, gq_ref, gk_ref, gv_ref, gg_ref, gk_st, gv_st, r_st, fall, k_ref, v_ref) = refs[6:17]
     (
-        crow, rise, fall, dec, w_st, p_st, g_st, a_st, su_st, da_st, gk_st, gv_st, own_st, s_st, r_st, ggp,
-        zout, zin, zs, zr,
-    ) = refs[11:31]
+        q_ref, log_ref, gain_ref, u_ref, crow, rise, dec, w_st, p_st, g_st, a_st, su_st, da_st, own_st, s_st,
+        zout, zin, zs, zr, load_sem,
+    ) = refs[17:37]
     ctx = lax.axis_index("ctx")
     tp = lax.axis_index("tp")
     core = ctx % 2
@@ -99,8 +143,8 @@
     p = chip % CHIPS
     g = chip // CHIPS
     place = (core, p, g, tp)
-    fwd = Scan(refs[31:51], place)
-    bwd = Scan(refs[51:71], place)
+    fwd = Scan(refs[37:57], place)
+    bwd = Scan(refs[57:77], place)
     first = core == 0
 
     def tp_copy(d, arriving=False):
@@ -111,6 +155,21 @@
             device_id=(ctx, peer), device_id_type=MESH,
         )
 
+    def half_load(src, dst, which, at):
+        columns = pl.ds(pl.multiple_of(which * 2 * DH, 2 * DH), 2 * DH)
+        return pltpu.make_async_copy(src.at[:, columns], dst.at[:, columns], load_sem.at[at])
+
+    log_load = pltpu.make_async_copy(log_hbm, log_ref, load_sem.at[0])
+    far_loads = [half_load(k_hbm, k_ref, 1 - core, 1), half_load(v_hbm, v_ref, 1 - core, 2)]
+    near_loads = [half_load(k_hbm, k_ref, core, 3), half_load(v_hbm, v_ref, core, 4)]
+    late_loads = [
+        pltpu.make_async_copy(q_hbm, q_ref, load_sem.at[5]),
+        pltpu.make_async_copy(u_hbm, u_ref, load_sem.at[6]),
+        pltpu.make_async_copy(gain_hbm, gain_ref, load_sem.at[7]),
+    ]
+    for load in [log_load] + far_loads + near_loads + late_loads:
+        load.start()
+
     barrier = pltpu.get_barrier_semaphore()
     partners = [fwd.device(g, p, 1 - core)]
     partners += [fwd.device(g, (p + d) % CHIPS, core) for d in range(1, CHIPS)]
@@ -119,6 +178,7 @@
     for partner in partners:
         pl.semaphore_signal(barrier, inc=1, device_id=partner, device_id_type=MESH)
 
+    log_load.wait()
     cum = log_ref[...]
     lane = lax.broadcasted_iota(jnp.int32, cum.shape, 1)
     step = 1
@@ -163,12 +223,16 @@
 
     mine = 2 * core
     other = 2 * (1 - core)
+    for load in far_loads:
+        load.wait()
     for j in range(2):
         fwd.out0[j * DH : (j + 1) * DH, :] = keyed_state(other + j)
         fwd.out0[2 * DH + j : 2 * DH + j + 1, :] = dec[other + j]
     fwd.out0[2 * DH + 2 : 2 * DH + 8, :] = jnp.zeros((6, DH), F32)
     pl.semaphore_wait(barrier, len(partners))
     fwd.copy0().start()
+    for load in near_loads:
+        load.wait()
     for j in range(2):
         own_st[j] = keyed_state(mine + j)
 
@@ -290,18 +354,11 @@
             gv_st[cols, lanes(h)] = mm(p_st[h, below, cols], da_st[below, lanes(h)], 0, 0)
 
     def finish(h):
-        hi, lo = split(r_st[h])
-        for rb in range(NRB):
-            rows = slice(rb * ROWB, (rb + 1) * ROWB)
-            vv, kk, down = v_ref[rows, lanes(h)], k_ref[rows, lanes(h)], fall[h, rows, :]
-            gk_ref[rows, lanes(h)] = (
-                gk_st[rows, lanes(h)] + down * (mm(vv, hi, 1, 1) + mm(vv, lo, 1, 1))
-            ).astype(BF16)
-            gv_ref[rows, lanes(h)] = (
-                gv_st[rows, lanes(h)] + down * (mm(kk, hi, 1, 0) + mm(kk, lo, 1, 0))
-            ).astype(BF16)
+        finish_head(lanes(h), r_st[h], fall.at[h], v_ref, k_ref, gk_st, gv_st, gk_ref, gv_ref)
 
     send_chip(fwd, False)
+    for load in late_loads:
+        load.wait()
     intra_forward(0)
     intra_forward(1)
     send_group(fwd, False)
@@ -377,7 +434,6 @@
     bwd.copy4().wait()
     for j in range(2):
         r_st[other + j] = bwd.in4[j]
-        finish(other + j)
 
     for scan in (fwd, bwd):
         for d in range(1, CHIPS):
@@ -412,9 +468,16 @@
     vmem = pl.BlockSpec(memory_space=pltpu.VMEM)
     big = jax.ShapeDtypeStruct((BLK, HEADS * DH), BF16)
     dma = pltpu.SemaphoreType.DMA
+    row = jax.ShapeDtypeStruct((1, HEADS * DH), F32)
+    full = jax.ShapeDtypeStruct((BLK, HEADS * DH), F32)
+    states = jax.ShapeDtypeStruct((HEADS, DH, DH), F32)
+    columns = jax.ShapeDtypeStruct((HEADS, BLK, DH), F32)
     scratch = [
+        pltpu.VMEM((BLK, HEADS * DH), BF16),
+        pltpu.VMEM((HEADS, BLK), F32),
+        pltpu.VMEM((1, HEADS * DH), F32),
+        pltpu.VMEM((BLK, HEADS * DH), BF16),
         pltpu.VMEM((HEADS, 1, BLK), F32),
-        pltpu.VMEM((HEADS, BLK, DH), F32),
         pltpu.VMEM((HEADS, BLK, DH), F32),
         pltpu.VMEM((HEADS, 1, DH), F32),
         pltpu.VMEM((HEADS, BLK, BLK), F32),
@@ -423,28 +486,39 @@
         pltpu.VMEM((BLK, HEADS * DH), F32),
         pltpu.VMEM((BLK, HEADS * DH), F32),
         pltpu.VMEM((BLK, HEADS * DH), BF16),
-        pltpu.VMEM((BLK, HEADS * DH), F32),
-        pltpu.VMEM((BLK, HEADS * DH), F32),
         pltpu.VMEM((2, DH, DH), F32),
         pltpu.VMEM((HEADS, DH, DH), F32),
-        pltpu.VMEM((HEADS, DH, DH), F32),
-        pltpu.VMEM((8, DH), F32),
         pltpu.VMEM((8, DH), F32),
         pltpu.VMEM((TP, 8, DH), F32),
         dma((TP,)),
         dma((TP,)),
+        dma((8,)),
     ]
-    attn, gq, gk, gv, gg = pl.pallas_call(
+    hbm = pl.BlockSpec(memory_space=pltpu.HBM)
+    held = pl.pallas_call(
         kernel,
-        out_shape=(big, big, big, big, jax.ShapeDtypeStruct((1, HEADS * DH), F32)),
-        in_specs=[vmem] * 6,
-        out_specs=(vmem,) * 5,
+        out_shape=(big, big, big, big, row, full, full, states, columns, big, big),
+        in_specs=[hbm] * 6,
+        out_specs=(vmem,) * 11,
         scratch_shapes=scratch + scan_scratch() + scan_scratch(),
         compiler_params=pltpu.CompilerParams(
             collective_id=0, has_side_effects=True, vmem_limit_bytes=40 * 2**20
         ),
         name="attention",
-    )(queries, keys, values, log_decay.T, gain.reshape(1, HEADS * DH), upstream)
+    )(*(pltpu.with_memory_space_constraint(x, pltpu.HBM) for x in (queries, keys, values, log_decay.T, gain.reshape(1, HEADS * DH), upstream)))
+    attn, gq, gk, gv, gg = pl.pallas_call(
+        tail_kernel,
+        out_shape=(big, big, big, big, row),
+        in_specs=[vmem] * 11,
+        out_specs=(hbm,) * 5,
+        scratch_shapes=[
+            pltpu.VMEM((BLK, HEADS * DH), BF16),
+            pltpu.VMEM((BLK, HEADS * DH), BF16),
+            dma((7,)),
+        ],
+        compiler_params=pltpu.CompilerParams(vmem_limit_bytes=24 * 2**20),
+        name="finish",
+    )(*held)
     return attn, gq, gk, gv, gg.reshape(HEADS * DH)
 
 

time: 65.1 us -> 57 us (0.88)
  local copies, waits for them, and re-layouts: 9.29 us -> 0 us
  Pallas kernels: 54.8 us -> 56.2 us
    unnamed x17 -> x0, local copies, waits for them, and re-layouts: 9.29 us -> none
    pallas_call x1 -> x2, Pallas kernels: 54.8 us -> 56.2 us  [the longest x1 54.3 us: body(): pl.pallas_call(kernel, out_shape=(big, big, big, big, row, full, full, st...]
where the time goes in v2:
time: 57 us; the launch traced here: 56.8 us
  Pallas kernels  56.2 us (99%)
  between operations  0.64 us (1%)
    pallas_call x1, Pallas kernels, body(): pl.pallas_call(kernel, out_shape=(big, big, big, big, row, full, full, st...  54.3 us
    pallas_call x1, Pallas kernels, body(): pl.pallas_call(tail_kernel, out_shape=(big, big, big, big, row), in_specs...  1.87 us

profile of v2, /device:TPU:1, one launch (start us, length us, event | category | flops | bytes accessed | tf_op | source)
XLA Modules:
  0.0 56.8 jit_solution(176999122181052210)
XLA Ops:
  0.6 54.3 %attention.1 = (bf16[512,512]{1,0:T(8,128)(2,1)S(1)}, bf16[512,512]{1,0:T(8,128)(2,1)S(1)}, bf16[512,512]{1,0:T(8,128)(2,1)S(1)}, bf16[512,512]{1,0:T(8,128)(2,1...) custom-call(bf16[512,512]{1,0:T(8,128)(2,1)} %refs_0_.1, ...), custom_call_target="tpu_custom_call" | custom-call | tf_op jit(solution)/shard_map/attention/pallas_call | solution.py:498
  54.9 1.9 %finish.1 = (bf16[512,512]{1,0:T(8,128)(2,1)}, bf16[512,512]{1,0:T(8,128)(2,1)}, bf16[512,512]{1,0:T(8,128)(2,1)}, bf16[512,512]{1,0:T(8,128)(2,1)}, f32[1,512]{1,0:T(1,128)}) custom-call(bf16[512,512]{1,0:T(8,128)(2,1)S(1)} %get-tuple-element.21.out_in, bf16[512,512]{1,0:T(8,128)(2,1)S(1)} %get-tuple-element.22.gq_in, ...), custom_call_target="tpu_custom_call" | custom-call | tf_op jit(solution)/shard_map/finish/pallas_call | solution.py:509
